TPU v7x, 32 devices: a whole 2x2x4 slice. The times are simulated.
32 devices in a mesh: dp: 8 (over z, core), tensor: 4 (over y, x).
Axes of the slice: x: 2, y: 2, z: 4, core: 2. Of those that a mesh axis runs over, the one named last changes fastest.
Arguments:
- policy: bfloat16 [8, 1024, 16384], P('dp', 'tensor'), may hold values from -4 to 4
- ref_weight: bfloat16 [8192, 16384], P('tensor', 'dp'), may hold values from -4 to 4
- tokens: bfloat16 [2, 384, 8192], P(None, 'dp', 'tensor'), may hold values from -400 to 400
- gain: float32 [8192], P('tensor'), may hold values from 0.5 to 2
Outputs:
- blended: bfloat16 [8192, 16384], P('tensor', 'dp')
- activated: bfloat16 [2, 384, 16384], P(None, 'tensor', 'dp')
All inputs are finite; a program needn't handle non-finite values.
Results may differ from a plain program's by a relative error of at most 0.022.
Values may be sent and summed in bfloat16 or wider, within the bound.
A program may use at most 128 MiB of HBM per device.

v0:
```python
import math

import jax
import jax.numpy as jnp
from jax import lax
from jax.sharding import PartitionSpec as P

D = 8192


ema_rate = 0.5
norm_eps = 1e-06


def body(policy, ref_weight, tokens, gain):
    arrived = lax.all_to_all(policy, "dp", split_axis=2, concat_axis=0, tiled=True)
    piece_count, piece_rows, piece_cols = arrived.shape
    policy_slice = arrived.reshape(piece_count * piece_rows, piece_cols)
    ref_f = ref_weight.astype(jnp.float32)
    blended = (ref_f + ema_rate * (policy_slice.astype(jnp.float32) - ref_f)).astype(jnp.bfloat16)
    out_scale = 1.0 / math.sqrt(D)
    tensor_count = lax.axis_size("tensor")

    def partial_maker(all_rows):
        micro_count, gath_rows, local_width = all_rows.shape
        per_device = gath_rows // tensor_count
        blocked = all_rows.reshape(micro_count, tensor_count, per_device, local_width)
        span_rows = micro_count * per_device

        def partial_term(first_row, row_count):
            block_count = row_count // span_rows
            flat_rows = jnp.transpose(blocked, (1, 0, 2, 3)).reshape(
                block_count * span_rows, local_width
            )
            return jnp.dot(flat_rows, blended, preferred_element_type=jnp.float32) * out_scale

        return (partial_term, span_rows, per_device)

    pieces = []
    for micro in range(tokens.shape[0]):
        normed_tok_block = tokens[micro : micro + 1]
        tok_f = normed_tok_block.astype(jnp.float32)
        normed_row_total = lax.psum(jnp.sum(tok_f * tok_f, axis=2), "tensor")
        scaled = (
            normed_tok_block.astype(jnp.float32)
            * lax.rsqrt(normed_row_total / D + norm_eps)[..., None]
        )
        all_rows = lax.all_gather((scaled * gain).astype(jnp.bfloat16), "dp", axis=1, tiled=True)
        partial_term, dev_rows, per_device = partial_maker(all_rows)
        summed = lax.psum_scatter(
            partial_term(jnp.int32(0), dev_rows * lax.axis_size("tensor")).astype(jnp.bfloat16),
            "tensor",
            scatter_dimension=0,
            tiled=True,
        ).astype(jnp.float32)
        pieces.append(summed.reshape(1, per_device, summed.shape[1]))
    gate = jnp.concatenate(pieces, axis=0)
    return (blended, jax.nn.silu(gate).astype(jnp.bfloat16))


def solution(mesh):
    return jax.shard_map(
        body,
        mesh=mesh,
        in_specs=(P("dp", "tensor", None), P("tensor", "dp"), P(None, "dp", "tensor"), P("tensor")),
        out_specs=(P("tensor", "dp"), P(None, "tensor", "dp")),
        check_vma=False,
    )
```

profile of v0, /device:TPU:13, one launch (start us, length us, event | category | flops | bytes accessed | tf_op | source)
XLA Modules:
  0.0 517.3 jit_solution(13677454782615517710)
XLA Ops:
  7.2 34.5 %copy.7 = bf16[1,256,16384]{1,0,2:T(2,128)(2,1)} copy(bf16[1,256,16384]{2,1,0:T(8,128)(2,1)} %param.4) | data formatting | bytes 16777216 | tf_op args[0]
  41.6 0.5 broadcast.26
  42.1 84.8 %reduce.2 = bf16[16384,256]{1,0:T(8,128)(2,1)} reduce(bf16[16384,1,256]{2,1,0:T(2,128)(2,1)} %bitcast.24, bf16[]{:T(256)} %broadcast.26), dimensions={1}, to_apply=%bitcast.20.reduce_sub_computation | reduce | bytes 16777218
  126.9 9.7 %reshape.33 = bf16[8,2,262144]{2,1,0:T(2,128)(2,1)} reshape(bf16[16384,256]{1,0:T(8,128)(2,1)} %reduce.2) | data formatting | bytes 16777216
  136.6 0.0 copy-start
  136.6 0.0 copy-start.1
  136.6 5.8 %all-to-all-start = ((bf16[8,2,262144]{2,1,0:T(2,128)(2,1)}), bf16[8,2,262144]{2,1,0:T(2,128)(2,1)}, u32[]{:S(2)}, u32[]{:S(2)}) async-start(bf16[8,2,262144]{2,1,0:T(2,128)(2,1)} %reshape.33), calls=%async_computation | async-start | bytes 16777216 | tf_op jit(solution)/shard_map/all_to_all | solution.py:16
  142.3 0.0 all-gather.5.cloned.1.call-start
  142.3 0.0 copy-done
  142.4 0.2 fusion.8
  142.5 7.7 %all-reduce = (f32[1,48]{1,0:T(1,128)S(1)}, f32[1,48]{1,0:T(1,128)S(1)}) all-reduce(f32[1,48]{1,0:T(1,128)S(1)} %bitcast.29, f32[1,48]{1,0:T(1,128)S(1)} %bitcast.28), channel_id=1, replica_groups=mesh['dp'=8,'tensor'=4] {'tensor'}, use_global_device_ids=true, to_apply=%region_4.0 | all-reduce | flops 96 | bytes 768 | tf_op jit(solution)/shard_map/psum | solution.py:43
  150.3 0.0 copy-done.1
  150.3 0.9 fusion.10
  151.2 0.0 all-gather.5.cloned.1.call-update
  151.2 0.0 all-gather.3.cloned.1.call-start
  151.3 0.7 all-gather.3.cloned.1.call-update
  152.0 0.0 reduce-scatter.5.cloned.1.call-start
  152.0 195.9 %all-to-all-done = bf16[8,2,262144]{2,1,0:T(2,128)(2,1)} async-done(((bf16[8,2,262144]{2,1,0:T(2,128)(2,1)}), bf16[8,2,262144]{2,1,0:T(2,128)(2,1)}, u32[]{:S(2)}, u32[]{:S(2)}) %all-to-all-start) | async-done | bytes 8388640 | tf_op jit(solution)/shard_map/all_to_all | solution.py:16
  348.0 13.3 %reshape.34 = bf16[16384,1,256]{2,1,0:T(2,128)(2,1)} reshape(bf16[8,2,262144]{2,1,0:T(2,128)(2,1)} %all-to-all-done) | data formatting | bytes 16777216
  361.3 19.9 %convert_bitcast_fusion = f32[8,1,256,2048]{2,1,3,0:T(1,128)} fusion(bf16[1,256,8,2048]{1,0,3,2:T(2,128)(2,1)} %bitcast.25), kind=kLoop, calls=%fused_computation.4 | loop fusion | flops 4194304 | bytes 25165824 | tf_op jit(solution)/shard_map/convert_element_type | solution.py:20
  381.2 40.1 %copy.8 = f32[8,1,256,2048]{3,2,0,1:T(8,128)} copy(f32[8,1,256,2048]{2,1,3,0:T(1,128)} %convert_bitcast_fusion) | data formatting | bytes 33554432 | tf_op jit(solution)/shard_map/convert_element_type | solution.py:20
  421.3 12.0 %fusion.1 = bf16[2048,2048]{1,0:T(8,128)(2,1)} fusion(bf16[2048,2048]{1,0:T(8,128)(2,1)} %param.5, f32[8,1,256,2048]{3,2,0,1:T(8,128)} %copy.8), kind=kLoop, calls=%fused_computation.3 | loop fusion | flops 20971520 | bytes 33554432 | tf_op jit(solution)/shard_map/convert_element_type | solution.py:20
  433.3 0.0 all-gather.5.cloned.1.call-done
  433.3 8.5 %multiply_convert_fusion = bf16[384,2048]{1,0:T(8,128)(2,1)} fusion(bf16[2048,2048]{1,0:T(8,128)(2,1)} %fusion.1, bf16[1,384,2048]{2,1,0:T(8,128)(2,1)} %all-gather.5.cloned.1.call-done), kind=kOutput, calls=%fused_computation.5 | convolution fusion | flops 3222798336 | bytes 11534336 | tf_op jit(solution)/shard_map/dot_general | solution.py:35
  441.8 0.0 reduce-scatter.5.cloned.1.call-update
  441.8 0.2 reduce-scatter.3.cloned.1.call-start
  442.0 0.0 all-gather.3.cloned.1.call-done
  442.1 8.4 %multiply_convert_fusion.1 = bf16[384,2048]{1,0:T(8,128)(2,1)} fusion(bf16[2048,2048]{1,0:T(8,128)(2,1)} %fusion.1, bf16[1,384,2048]{2,1,0:T(8,128)(2,1)} %all-gather.3.cloned.1.call-done), kind=kOutput, calls=%fused_computation.6 | convolution fusion | flops 3222798336 | bytes 11534336 | tf_op jit(solution)/shard_map/dot_general | solution.py:35
  450.5 0.0 reduce-scatter.3.cloned.1.call-update
  450.5 24.0 %reduce-scatter.5.cloned.1.call-done = bf16[96,2048]{1,0:T(8,128)(2,1)} async-done(((bf16[384,2048]{1,0:T(8,128)(2,1)}), bf16[96,2048]{1,0:T(8,128)(2,1)}) %reduce-scatter.5.cloned.1.call-update) | async-done | bytes 393232 | tf_op jit(solution)/shard_map/reduce_scatter | solution.py:50
  474.5 33.8 %reduce-scatter.3.cloned.1.call-done = bf16[96,2048]{1,0:T(8,128)(2,1)} async-done(((bf16[384,2048]{1,0:T(8,128)(2,1)}), bf16[96,2048]{1,0:T(8,128)(2,1)}) %reduce-scatter.3.cloned.1.call-update) | async-done | bytes 393232 | tf_op jit(solution)/shard_map/reduce_scatter | solution.py:50
  508.3 2.4 fusion.5
  (1 shorter events, 0.0 us)
Async XLA Ops:
  136.6 5.8 %copy-start = (bf16[2,48,2048]{2,1,0:T(8,128)(2,1)S(1)}, bf16[2,48,2048]{2,1,0:T(8,128)(2,1)}, u32[]{:S(2)}) copy-start(bf16[2,48,2048]{2,1,0:T(8,128)(2,1)} %param.6) | copy-start | bytes 1179652
  136.6 13.7 %copy-start.1 = (f32[2048]{0:T(1024)S(1)}, f32[2048]{0:T(1024)}, u32[]{:S(2)}) copy-start(f32[2048]{0:T(1024)} %param.7) | copy-start | bytes 24580
  136.6 211.4 %all-to-all-start = ((bf16[8,2,262144]{2,1,0:T(2,128)(2,1)}), bf16[8,2,262144]{2,1,0:T(2,128)(2,1)}, u32[]{:S(2)}, u32[]{:S(2)}) async-start(bf16[8,2,262144]{2,1,0:T(2,128)(2,1)} %reshape.33), calls=%async_computation | async-start | bytes 16777216 | tf_op jit(solution)/shard_map/all_to_all | solution.py:16
  142.3 291.0 %all-gather.5.cloned.1.call-start = ((), (), s32[]{:S(2)}) async-start(), calls=%async_computation.5 | async-start | bytes 1769472 | tf_op jit(solution)/shard_map/all_gather | solution.py:48
  151.2 290.8 %all-gather.3.cloned.1.call-start = ((), (), s32[]{:S(2)}) async-start(), calls=%async_computation.3 | async-start | bytes 1769472 | tf_op jit(solution)/shard_map/all_gather | solution.py:48
  152.0 322.6 %reduce-scatter.5.cloned.1.call-start = ((), (), s32[]{:S(2)}) async-start(), calls=%async_computation.6 | async-start | bytes 1966080 | tf_op jit(solution)/shard_map/reduce_scatter | solution.py:50
  441.8 66.5 %reduce-scatter.3.cloned.1.call-start = ((), (), s32[]{:S(2)}) async-start(), calls=%async_computation.4 | async-start | bytes 1966080 | tf_op jit(solution)/shard_map/reduce_scatter | solution.py:50
Sparse Core Ops, SparseCore 0:
  151.3 38.5 all-gather.4
  192.1 46.5 all-gather.2
  441.9 32.5 reduce-scatter.4
  477.4 30.8 reduce-scatter.2
where the time goes:
time: 522 us; the launch traced here: 517 us
  waiting for transfers between devices  254 us (49%)
  other arithmetic  120 us (23%)
  local copies, waits for them, and re-layouts  98.1 us (19%)
  matrix products  16.9 us (3%)
  between operations  13.8 us (3%)
  blocking collectives  7.74 us (1%)
  starting transfers between devices  6.07 us (1%)
    all_to_all x1, waiting for transfers between devices, body(): lax.all_to_all(policy, 'dp', split_axis=2, concat_axis=0, tiled=True)  196 us
    unnamed x1, other arithmetic  84.8 us
    unnamed x8, local copies, waits for them, and re-layouts  57.9 us
    reduce_scatter x2, waiting for transfers between devices, body(): lax.psum_scatter(partial_term(jnp.int32(0), dev_rows * lax.axis_size('ten...  57.8 us
    convert_element_type x1, local copies, waits for them, and re-layouts, body(): policy_slice.astype(jnp.float32) - ref_f  40.1 us
    convert_element_type x1, other arithmetic, body(): policy_slice.astype(jnp.float32) - ref_f  19.9 us
    dot_general x2, matrix products, partial_term(): jnp.dot(flat_rows, blended, preferred_element_type=jnp.float32) * out_scale  16.9 us
    convert_element_type x1, other arithmetic, body(): (ref_f + ema_rate * (policy_slice.astype(jnp.float32) - ref_f)).astype(jn...  12 us
  transfers between devices with their start and end apart: 5, of which 3 were waited for; matrix products, arithmetic and copies ran while one was open for 20% of the time, Pallas kernels for 0%

commit v1 on v0

v1 whole, which is shorter than its diff:
```python
import functools
import math

import jax
import jax.numpy as jnp
from jax import lax
from jax.experimental import pallas as pl
from jax.experimental.pallas import tpu as pltpu
from jax.sharding import PartitionSpec as P

MESH = pl.DeviceIdType.MESH
LANES = 128
AHEAD = 2

ema_rate = 0.5
norm_eps = 1e-06


def each(count, step):
    lax.fori_loop(0, count, lambda i, _: (step(i), 0)[1], 0)


def fused_kernel(
    plan,
    policy,
    ref_in,
    tokens,
    gain,
    blended,
    activated,
    arrived,
    weights,
    tok,
    squares,
    gathered,
    partial,
    terms,
    piece_send,
    piece_recv,
    own_sem,
    ref_sem,
    out_sem,
    tok_sem,
    square_send,
    square_recv,
    up_send,
    down_send,
    pair_send,
    block_recv,
    term_send,
    term_recv,
):
    dp, tensor, chunks, width, model = plan
    me = lax.axis_index("dp")
    col = lax.axis_index("tensor")
    levels = dp // 2
    level = me // 2
    core = me % 2
    pair = me + 1 - 2 * core
    per_owner = dp // tensor
    micros, per_micro, features = tokens.shape
    rows = micros * per_micro
    columns = chunks * width

    barrier = pltpu.get_barrier_semaphore()
    for off in range(1, dp):
        pl.semaphore_signal(
            barrier, inc=1, device_id={"dp": (me + off) % dp}, device_id_type=MESH
        )
    for off in range(1, tensor):
        pl.semaphore_signal(
            barrier, inc=1, device_id={"tensor": (col + off) % tensor}, device_id_type=MESH
        )

    def own_piece(c):
        return pltpu.make_async_copy(
            policy.at[:, pl.ds(pl.multiple_of(me * columns + c * width, width), width)],
            arrived.at[c, me],
            own_sem.at[c],
        )

    def ref_piece(c):
        return pltpu.make_async_copy(
            ref_in.at[:, :, pl.ds(pl.multiple_of(c * width, width), width)],
            weights.at[c],
            ref_sem.at[c],
        )

    def out_piece(c):
        return pltpu.make_async_copy(
            weights.at[c],
            blended.at[:, :, pl.ds(pl.multiple_of(c * width, width), width)],
            out_sem.at[c],
        )

    def send_piece(c, other):
        return pltpu.make_async_remote_copy(
            src_ref=policy.at[
                :, pl.ds(pl.multiple_of(other * columns + c * width, width), width)
            ],
            dst_ref=arrived.at[c, me],
            send_sem=piece_send.at[c, other],
            recv_sem=piece_recv.at[c, me],
            device_id={"dp": other},
            device_id_type=MESH,
        )

    def take_piece(c, other):
        return pltpu.make_async_remote_copy(
            src_ref=policy.at[:, pl.ds(0, width)],
            dst_ref=arrived.at[c, other],
            send_sem=piece_send.at[c, other],
            recv_sem=piece_recv.at[c, other],
            device_id={"dp": other},
            device_id_type=MESH,
        )

    def send_squares(other):
        return pltpu.make_async_remote_copy(
            src_ref=squares.at[col],
            dst_ref=squares.at[col],
            send_sem=square_send.at[other],
            recv_sem=square_recv.at[col],
            device_id={"tensor": other},
            device_id_type=MESH,
        )

    def take_squares(other):
        return pltpu.make_async_remote_copy(
            src_ref=squares.at[other],
            dst_ref=squares.at[other],
            send_sem=square_send.at[other],
            recv_sem=square_recv.at[other],
            device_id={"tensor": other},
            device_id_type=MESH,
        )

    def block_copy(block, sem, other):
        return pltpu.make_async_remote_copy(
            src_ref=gathered.at[block],
            dst_ref=gathered.at[block],
            send_sem=sem,
            recv_sem=block_recv.at[block],
            device_id={"dp": other},
            device_id_type=MESH,
        )

    def send_term(c, other):
        return pltpu.make_async_remote_copy(
            src_ref=partial.at[c, pl.ds(other * per_owner, per_owner)],
            dst_ref=terms.at[c, col],
            send_sem=term_send.at[c, other],
            recv_sem=term_recv.at[c, col],
            device_id={"tensor": other},
            device_id_type=MESH,
        )

    def take_term(c, other):
        return pltpu.make_async_remote_copy(
            src_ref=partial.at[c, pl.ds(other * per_owner, per_owner)],
            dst_ref=terms.at[c, other],
            send_sem=term_send.at[c, other],
            recv_sem=term_recv.at[c, other],
            device_id={"tensor": other},
            device_id_type=MESH,
        )

    tok_copy = pltpu.make_async_copy(tokens, tok, tok_sem)
    tok_copy.start()
    each(chunks, lambda c: ref_piece(c).start())
    each(chunks, lambda c: own_piece(c).start())
    tok_copy.wait()
    for m in range(micros):
        total = jnp.zeros((per_micro, LANES), jnp.float32)
        for f in range(features // LANES):
            part = tok[m, :, f * LANES : (f + 1) * LANES].astype(jnp.float32)
            total = total + part * part
        squares[col, m * per_micro : (m + 1) * per_micro, :] = total
    pl.semaphore_wait(barrier, dp + tensor - 2)

    for off in range(1, tensor):
        send_squares((col + off) % tensor).start()

    order = sorted(range(1, dp), key=lambda off: abs(off - dp // 2))

    def send_chunk(c):
        for off in order:
            send_piece(c, (me + off) % dp).start()

    for c in range(AHEAD):
        send_chunk(c)

    for off in range(1, tensor):
        take_squares((col + off) % tensor).wait_recv()
    for m in range(micros):
        total = squares[0, m * per_micro : (m + 1) * per_micro, :]
        for t in range(1, tensor):
            total = total + squares[t, m * per_micro : (m + 1) * per_micro, :]
        scale = lax.rsqrt(jnp.sum(total, axis=1, keepdims=True) / model + norm_eps)
        for f in range(0, features, 512):
            span = min(512, features - f)
            gathered[me, m * per_micro : (m + 1) * per_micro, f : f + span] = (
                tok[m, :, f : f + span].astype(jnp.float32) * scale * gain[:, f : f + span]
            ).astype(jnp.bfloat16)

    def relay(step, act):
        below = level - step
        above = level + step

        @pl.when(below >= 0)
        def _():
            block = 2 * below + core
            if step > 0:
                act("take", block_copy(block, up_send.at[step], me))

            @pl.when(level + 1 < levels)
            def _():
                act("send", block_copy(block, up_send.at[step], (me + 2) % dp))

            act("send", block_copy(block, pair_send.at[below], pair))

        @pl.when(above < levels)
        def _():
            block = 2 * above + core
            if step > 0:
                act("take", block_copy(block, down_send.at[step], me))
                act("send", block_copy(block, pair_send.at[above], pair))

            @pl.when(level > 0)
            def _():
                act("send", block_copy(block, down_send.at[step], (me + dp - 2) % dp))

    def forward(kind, copy):
        copy.wait_recv() if kind == "take" else copy.start()

    def settle(kind, copy):
        if kind == "send":
            copy.wait_send()

    relay(0, forward)

    def take_chunk(c):
        ref_piece(c).wait()
        own_piece(c).wait()
        for off in range(1, dp):
            take_piece(c, (me + off) % dp).wait_recv()

        def blend(d):
            old = weights[c, d].astype(jnp.float32)
            new = arrived[c, d].astype(jnp.float32)
            weights[c, d] = (old + ema_rate * (new - old)).astype(jnp.bfloat16)

        each(dp, blend)
        out_piece(c).start()

    out_scale = 1.0 / math.sqrt(model)

    def multiply(c):
        left = gathered[...].reshape(dp * rows, features)
        right = weights[c].reshape(features, width)
        product = jnp.dot(left, right, preferred_element_type=jnp.float32) * out_scale
        partial[c] = product.astype(jnp.bfloat16).reshape(dp, rows, width)
        for off in range(1, tensor):
            send_term(c, (col + off) % tensor).start()

    def finish(c):
        for off in range(1, tensor):
            take_term(c, (col + off) % tensor).wait_recv()
        for b in range(per_owner):
            gate = partial[c, col * per_owner + b].astype(jnp.float32)
            for off in range(1, tensor):
                gate = gate + terms[c, (col + off) % tensor, b].astype(jnp.float32)
            result = (gate / (1.0 + jnp.exp(-gate))).astype(jnp.bfloat16)
            for m in range(micros):
                activated[
                    m,
                    pl.ds(b * per_micro, per_micro),
                    pl.ds(pl.multiple_of(c * width, width), width),
                ] = result[m * per_micro : (m + 1) * per_micro]

    early = levels
    for c in range(early):
        if c + AHEAD < chunks:
            send_chunk(c + AHEAD)
        take_chunk(c)
        if c + 1 < levels:
            relay(c + 1, forward)
    each(levels, lambda z: block_copy(2 * z + 1 - core, pair_send.at[z], pair).wait_recv())
    each(early, multiply)

    def late(c):
        c = c + early

        @pl.when(c + AHEAD < chunks)
        def _():
            send_chunk(c + AHEAD)

        take_chunk(c)
        multiply(c)
        finish(c - early)

    each(chunks - early, late)
    each(early, lambda c: finish(c + chunks - early))

    for off in range(1, tensor):
        send_squares((col + off) % tensor).wait_send()
    for step in range(levels):
        relay(step, settle)

    def settle_chunk(c):
        out_piece(c).wait()
        for off in range(1, dp):
            send_piece(c, (me + off) % dp).wait_send()
        for off in range(1, tensor):
            send_term(c, (col + off) % tensor).wait_send()

    each(chunks, settle_chunk)


def fused(policy, ref_weight, tokens, gain, dp, tensor, chunks, model):
    _, piece_rows, _ = policy.shape
    local, columns = ref_weight.shape
    micros, per_micro, features = tokens.shape
    rows = micros * per_micro
    per_owner = dp // tensor
    width = columns // chunks
    bf16, f32 = jnp.bfloat16, jnp.float32
    plan = (dp, tensor, chunks, width, model)
    dma = pltpu.SemaphoreType.DMA
    blended, activated = pl.pallas_call(
        functools.partial(fused_kernel, plan),
        out_shape=[
            jax.ShapeDtypeStruct((dp, piece_rows, columns), bf16),
            jax.ShapeDtypeStruct((micros, per_owner * per_micro, columns), bf16),
        ],
        in_specs=[
            pl.BlockSpec(memory_space=pl.ANY),
            pl.BlockSpec(memory_space=pl.ANY),
            pl.BlockSpec(memory_space=pl.ANY),
            pl.BlockSpec(memory_space=pltpu.VMEM),
        ],
        out_specs=[
            pl.BlockSpec(memory_space=pl.ANY),
            pl.BlockSpec(memory_space=pltpu.VMEM),
        ],
        scratch_shapes=[
            pltpu.VMEM((chunks, dp, piece_rows, width), bf16),
            pltpu.VMEM((chunks, dp, piece_rows, width), bf16),
            pltpu.VMEM((micros, per_micro, features), bf16),
            pltpu.VMEM((tensor, rows, LANES), f32),
            pltpu.VMEM((dp, rows, features), bf16),
            pltpu.VMEM((chunks, dp, rows, width), bf16),
            pltpu.VMEM((chunks, tensor, per_owner, rows, width), bf16),
            dma((chunks, dp)),
            dma((chunks, dp)),
            dma((chunks,)),
            dma((chunks,)),
            dma((chunks,)),
            dma,
            dma((tensor,)),
            dma((tensor,)),
            dma((dp // 2,)),
            dma((dp // 2,)),
            dma((dp // 2,)),
            dma((dp,)),
            dma((chunks, tensor)),
            dma((chunks, tensor)),
        ],
        compiler_params=pltpu.CompilerParams(
            collective_id=0, has_side_effects=True, vmem_limit_bytes=52 * 1024 * 1024
        ),
        cost_estimate=pl.CostEstimate(
            flops=2 * dp * rows * features * columns,
            bytes_accessed=10 * local * columns,
            transcendentals=per_owner * rows * columns,
        ),
    )(
        policy.reshape(piece_rows, dp * columns),
        ref_weight.reshape(dp, piece_rows, columns),
        tokens,
        gain.reshape(1, features),
    )
    return blended.reshape(local, columns), activated


def plain(policy, ref_weight, tokens, gain, tensor, model):
    arrived = lax.all_to_all(policy, "dp", split_axis=2, concat_axis=0, tiled=True)
    new = arrived.reshape(ref_weight.shape).astype(jnp.float32)
    old = ref_weight.astype(jnp.float32)
    blended = (old + ema_rate * (new - old)).astype(jnp.bfloat16)
    pieces = []
    for micro in range(tokens.shape[0]):
        values = tokens[micro].astype(jnp.float32)
        total = lax.psum(jnp.sum(values * values, axis=1, keepdims=True), "tensor")
        normed = (values * lax.rsqrt(total / model + norm_eps) * gain).astype(jnp.bfloat16)
        normed = lax.all_gather(normed, "dp", axis=0, tiled=True)
        term = jnp.dot(normed, blended, preferred_element_type=jnp.float32)
        term = (term * (1.0 / math.sqrt(model))).astype(jnp.bfloat16)
        pieces.append(lax.psum_scatter(term, "tensor", scatter_dimension=0, tiled=True))
    gate = jnp.stack(pieces).astype(jnp.float32)
    return blended, jax.nn.silu(gate).astype(jnp.bfloat16)


def solution(mesh):
    dp, tensor = mesh.shape["dp"], mesh.shape["tensor"]

    def body(policy, ref_weight, tokens, gain):
        local, columns = ref_weight.shape
        model = local * tensor
        chunks = columns // 256
        fits = (
            dp % (2 * tensor) == 0
            and policy.shape[1] % 16 == 0
            and tokens.shape[1] % 16 == 0
            and columns % 256 == 0
            and chunks > dp // 2
            and dp // 2 >= AHEAD
        )
        if fits:
            return fused(policy, ref_weight, tokens, gain, dp, tensor, chunks, model)
        return plain(policy, ref_weight, tokens, gain, tensor, model)

    return jax.shard_map(
        body,
        mesh=mesh,
        in_specs=(P("dp", "tensor", None), P("tensor", "dp"), P(None, "dp", "tensor"), P("tensor")),
        out_specs=(P("tensor", "dp"), P(None, "tensor", "dp")),
        check_vma=False,
    )
```

time: 522 us -> 222 us (0.43)
  waiting for transfers between devices: 254 us -> 0 us
  Pallas kernels: 0 us -> 210 us
  other arithmetic: 120 us -> 0 us
  local copies, waits for them, and re-layouts: 98.1 us -> 11 us
  matrix products: 16.9 us -> 0 us
  between operations: 13.8 us -> 0.65 us
  blocking collectives: 7.74 us -> 0 us
  starting transfers between devices: 6.07 us -> 0 us
    pallas_call x0 -> x1, Pallas kernels: none -> 210 us  [fused(): pl.pallas_call(functools.partial(fused_kernel, plan), out_shape=[jax.Shap...]
    all_to_all x1 -> x0, waiting for transfers between devices: 196 us -> none  [body(): lax.all_to_all(policy, 'dp', split_axis=2, concat_axis=0, tiled=True)]
    unnamed x1 -> x0, other arithmetic: 84.8 us -> none
    reduce_scatter x2 -> x0, waiting for transfers between devices: 57.8 us -> none  [body(): lax.psum_scatter(partial_term(jnp.int32(0), dev_rows * lax.axis_size('ten...]
    unnamed x8 -> x6, local copies, waits for them, and re-layouts: 57.9 us -> 11 us
    convert_element_type x1 -> x0, local copies, waits for them, and re-layouts: 40.1 us -> none  [body(): policy_slice.astype(jnp.float32) - ref_f]
    convert_element_type x4 -> x0, other arithmetic: 35.3 us -> none  [the longest x1 19.9 us: body(): policy_slice.astype(jnp.float32) - ref_f]
    dot_general x2 -> x0, matrix products: 16.9 us -> none  [partial_term(): jnp.dot(flat_rows, blended, preferred_element_type=jnp.float32) * out_scale]
  transfers between devices with their start and end apart: 5 -> 0, of which waited for: 3 -> 0; matrix products, arithmetic and copies ran while one was open for 20% -> 0% of each run, Pallas kernels for 0% -> 0%
where the time goes in v1:
time: 222 us
  Pallas kernels  210 us (95%)
  local copies, waits for them, and re-layouts  11 us (5%)
    pallas_call x1, Pallas kernels, fused(): pl.pallas_call(functools.partial(fused_kernel, plan), out_shape=[jax.Shap...  210 us
    unnamed x6, local copies, waits for them, and re-layouts  11 us

profile of v1, /device:TPU:13, one launch (start us, length us, event | category | flops | bytes accessed | tf_op | source)
XLA Modules:
  0.0 221.9 jit_solution(17536711357800418286)
XLA Ops:
  0.6 0.0 copy-start
  0.6 1.0 copy-done
  1.6 0.0 copy-start.1
  1.6 0.7 copy-done.1
  2.3 210.3 %shard_map.59 = (bf16[8,256,2048]{2,1,0:T(8,128)(2,1)}, bf16[2,96,2048]{2,1,0:T(8,128)(2,1)S(1)}) custom-call(bf16[256,16384]{1,0:T(8,128)(2,1)} %bitcast.6, bf16[8,256,2048]{2,1,0:T(8,128)(2,1)} %bitcast.7, bf16[2,48,2048]{2,1,0:T(8,128)(2,1)S(1)} %copy-done, f32[1,2048]{1,0:T(1,128)S(1)} %bitcast.4), custom_call_target="tpu_custom_call" | custom-call | flops 6442450944 | bytes 41943040 | tf_op jit(solution)/shard_map/pallas_call | solution.py:330
  212.6 8.4 %copy.8 = bf16[2048,2048]{1,0:T(8,128)(2,1)} copy(bf16[2048,2048]{1,0:T(8,128)(2,1)} %bitcast.5) | data formatting | bytes 16777216
  221.1 0.9 copy.9
Async XLA Ops:
  0.6 1.0 copy-start
  1.6 0.7 copy-start.1

commit v2 on v1

--- a/solution.py
+++ b/solution.py
@@ -29,8 +29,8 @@
     blended,
     activated,
     arrived,
-    weights,
     tok,
+    gains,
     squares,
     gathered,
     partial,
@@ -39,8 +39,8 @@
     piece_recv,
     own_sem,
     ref_sem,
-    out_sem,
     tok_sem,
+    gain_sem,
     square_send,
     square_recv,
     up_send,
@@ -79,18 +79,12 @@
             own_sem.at[c],
         )
 
+    def part_of(c):
+        return pl.ds(pl.multiple_of(c * width, width), width)
+
     def ref_piece(c):
         return pltpu.make_async_copy(
-            ref_in.at[:, :, pl.ds(pl.multiple_of(c * width, width), width)],
-            weights.at[c],
-            ref_sem.at[c],
-        )
-
-    def out_piece(c):
-        return pltpu.make_async_copy(
-            weights.at[c],
-            blended.at[:, :, pl.ds(pl.multiple_of(c * width, width), width)],
-            out_sem.at[c],
+            ref_in.at[:, :, part_of(c)], blended.at[:, :, part_of(c)], ref_sem.at[c]
         )
 
     def send_piece(c, other):
@@ -166,10 +160,13 @@
         )
 
     tok_copy = pltpu.make_async_copy(tokens, tok, tok_sem)
+    gain_copy = pltpu.make_async_copy(gain, gains, gain_sem)
     tok_copy.start()
+    gain_copy.start()
     each(chunks, lambda c: ref_piece(c).start())
     each(chunks, lambda c: own_piece(c).start())
     tok_copy.wait()
+    gain_copy.wait()
     for m in range(micros):
         total = jnp.zeros((per_micro, LANES), jnp.float32)
         for f in range(features // LANES):
@@ -200,7 +197,7 @@
         for f in range(0, features, 512):
             span = min(512, features - f)
             gathered[me, m * per_micro : (m + 1) * per_micro, f : f + span] = (
-                tok[m, :, f : f + span].astype(jnp.float32) * scale * gain[:, f : f + span]
+                tok[m, :, f : f + span].astype(jnp.float32) * scale * gains[:, f : f + span]
             ).astype(jnp.bfloat16)
 
     def relay(step, act):
@@ -242,22 +239,26 @@
     def take_chunk(c):
         ref_piece(c).wait()
         own_piece(c).wait()
-        for off in range(1, dp):
-            take_piece(c, (me + off) % dp).wait_recv()
 
         def blend(d):
-            old = weights[c, d].astype(jnp.float32)
+            old = blended[d, :, part_of(c)].astype(jnp.float32)
             new = arrived[c, d].astype(jnp.float32)
-            weights[c, d] = (old + ema_rate * (new - old)).astype(jnp.bfloat16)
-
-        each(dp, blend)
-        out_piece(c).start()
+            blended[d, :, part_of(c)] = (old + ema_rate * (new - old)).astype(jnp.bfloat16)
+
+        blend(me)
+
+        def take(i):
+            other = (me + i + 1) % dp
+            take_piece(c, other).wait_recv()
+            blend(other)
+
+        each(dp - 1, take)
 
     out_scale = 1.0 / math.sqrt(model)
 
     def multiply(c):
         left = gathered[...].reshape(dp * rows, features)
-        right = weights[c].reshape(features, width)
+        right = blended[:, :, part_of(c)].reshape(features, width)
         product = jnp.dot(left, right, preferred_element_type=jnp.float32) * out_scale
         partial[c] = product.astype(jnp.bfloat16).reshape(dp, rows, width)
         for off in range(1, tensor):
@@ -275,7 +276,7 @@
                 activated[
                     m,
                     pl.ds(b * per_micro, per_micro),
-                    pl.ds(pl.multiple_of(c * width, width), width),
+                    part_of(c),
                 ] = result[m * per_micro : (m + 1) * per_micro]
 
     early = levels
@@ -297,10 +298,12 @@
 
         take_chunk(c)
         multiply(c)
-        finish(c - early)
+        first = 2 * (c - early)
+        each(2, lambda i: pl.when(first + i < c)(lambda: finish(first + i)))
 
     each(chunks - early, late)
-    each(early, lambda c: finish(c + chunks - early))
+    done = min(2 * (chunks - early), chunks - 1)
+    each(chunks - done, lambda i: finish(done + i))
 
     for off in range(1, tensor):
         send_squares((col + off) % tensor).wait_send()
@@ -308,7 +311,6 @@
         relay(step, settle)
 
     def settle_chunk(c):
-        out_piece(c).wait()
         for off in range(1, dp):
             send_piece(c, (me + off) % dp).wait_send()
         for off in range(1, tensor):
@@ -334,19 +336,19 @@
             jax.ShapeDtypeStruct((micros, per_owner * per_micro, columns), bf16),
         ],
         in_specs=[
-            pl.BlockSpec(memory_space=pl.ANY),
-            pl.BlockSpec(memory_space=pl.ANY),
-            pl.BlockSpec(memory_space=pl.ANY),
-            pl.BlockSpec(memory_space=pltpu.VMEM),
+            pl.BlockSpec(memory_space=pltpu.HBM),
+            pl.BlockSpec(memory_space=pltpu.HBM),
+            pl.BlockSpec(memory_space=pltpu.HBM),
+            pl.BlockSpec(memory_space=pltpu.HBM),
         ],
         out_specs=[
-            pl.BlockSpec(memory_space=pl.ANY),
+            pl.BlockSpec(memory_space=pltpu.VMEM),
             pl.BlockSpec(memory_space=pltpu.VMEM),
         ],
         scratch_shapes=[
             pltpu.VMEM((chunks, dp, piece_rows, width), bf16),
-            pltpu.VMEM((chunks, dp, piece_rows, width), bf16),
             pltpu.VMEM((micros, per_micro, features), bf16),
+            pltpu.VMEM((1, features), f32),
             pltpu.VMEM((tensor, rows, LANES), f32),
             pltpu.VMEM((dp, rows, features), bf16),
             pltpu.VMEM((chunks, dp, rows, width), bf16),
@@ -355,7 +357,7 @@
             dma((chunks, dp)),
             dma((chunks,)),
             dma((chunks,)),
-            dma((chunks,)),
+            dma,
             dma,
             dma((tensor,)),
             dma((tensor,)),
@@ -367,7 +369,7 @@
             dma((chunks, tensor)),
         ],
         compiler_params=pltpu.CompilerParams(
-            collective_id=0, has_side_effects=True, vmem_limit_bytes=52 * 1024 * 1024
+            collective_id=0, has_side_effects=True, vmem_limit_bytes=40 * 1024 * 1024
         ),
         cost_estimate=pl.CostEstimate(
             flops=2 * dp * rows * features * columns,

time: 222 us -> 225 us (1.014)
  local copies, waits for them, and re-layouts: 11 us -> 14.2 us
    unnamed x6 -> x8, local copies, waits for them, and re-layouts: 11 us -> 14.2 us
where the time goes in v2:
time: 225 us
  Pallas kernels  210 us (93%)
  local copies, waits for them, and re-layouts  14.2 us (6%)
    pallas_call x1, Pallas kernels, fused(): pl.pallas_call(functools.partial(fused_kernel, plan), out_shape=[jax.Shap...  210 us
    unnamed x8, local copies, waits for them, and re-layouts  14.2 us

profile of v2, /device:TPU:13, one launch (start us, length us, event | category | flops | bytes accessed | tf_op | source)
XLA Modules:
  0.0 225.0 jit_solution(18254954026825358685)
XLA Ops:
  0.6 0.0 copy-start.1
  0.6 1.0 copy-done.1
  1.6 0.0 copy-start.2
  1.6 0.7 copy-done.2
  2.3 210.2 %shard_map.59 = (bf16[8,256,2048]{2,1,0:T(8,128)(2,1)S(1)}, bf16[2,96,2048]{2,1,0:T(8,128)(2,1)S(1)}) custom-call(bf16[256,16384]{1,0:T(8,128)(2,1)} %bitcast.6, bf16[8,256,2048]{2,1,0:T(8,128)(2,1)} %bitcast.7, bf16[2,48,2048]{2,1,0:T(8,128)(2,1)S(1)} %copy-done.1, f32[1,2048]{1,0:T(1,128)S(1)} %bitcast.5), custom_call_target="tpu_custom_call" | custom-call | flops 6442450944 | bytes 41943040 | tf_op jit(solution)/shard_map/pallas_call | solution.py:332
  212.5 0.0 copy-start
  212.5 3.2 %copy-done = bf16[8,256,2048]{2,1,0:T(8,128)(2,1)} copy-done((bf16[8,256,2048]{2,1,0:T(8,128)(2,1)}, bf16[8,256,2048]{2,1,0:T(8,128)(2,1)S(1)}, u32[]{:S(2)}) %copy-start) | copy-done | bytes 8388632
  215.7 8.4 %copy.8 = bf16[2048,2048]{1,0:T(8,128)(2,1)} copy(bf16[2048,2048]{1,0:T(8,128)(2,1)} %bitcast.4) | data formatting | bytes 16777216
  224.2 0.9 copy.9
Async XLA Ops:
  0.6 1.0 copy-start.1
  1.6 0.7 copy-start.2
  212.5 3.2 %copy-start = (bf16[8,256,2048]{2,1,0:T(8,128)(2,1)}, bf16[8,256,2048]{2,1,0:T(8,128)(2,1)S(1)}, u32[]{:S(2)}) copy-start(bf16[8,256,2048]{2,1,0:T(8,128)(2,1)S(1)} %get-tuple-element.4) | copy-start | bytes 25165828

commit v3 on v2

--- a/solution.py
+++ b/solution.py
@@ -11,6 +11,7 @@
 MESH = pl.DeviceIdType.MESH
 LANES = 128
 AHEAD = 2
+HOP_STEPS = 2
 
 ema_rate = 0.5
 norm_eps = 1e-06
@@ -184,8 +185,7 @@
         for off in order:
             send_piece(c, (me + off) % dp).start()
 
-    for c in range(AHEAD):
-        send_chunk(c)
+    send_chunk(0)
 
     for off in range(1, tensor):
         take_squares((col + off) % tensor).wait_recv()
@@ -235,6 +235,8 @@
             copy.wait_send()
 
     relay(0, forward)
+    for c in range(1, AHEAD):
+        send_chunk(c)
 
     def take_chunk(c):
         ref_piece(c).wait()
@@ -279,13 +281,15 @@
                     part_of(c),
                 ] = result[m * per_micro : (m + 1) * per_micro]
 
-    early = levels
+    early = HOP_STEPS * (levels - 1)
+    late_steps = chunks - early
+    per_step = -(-early // late_steps)
     for c in range(early):
         if c + AHEAD < chunks:
             send_chunk(c + AHEAD)
         take_chunk(c)
-        if c + 1 < levels:
-            relay(c + 1, forward)
+        if c % HOP_STEPS == 0:
+            relay(c // HOP_STEPS + 1, forward)
     each(levels, lambda z: block_copy(2 * z + 1 - core, pair_send.at[z], pair).wait_recv())
     each(early, multiply)
 
@@ -298,11 +302,11 @@
 
         take_chunk(c)
         multiply(c)
-        first = 2 * (c - early)
-        each(2, lambda i: pl.when(first + i < c)(lambda: finish(first + i)))
-
-    each(chunks - early, late)
-    done = min(2 * (chunks - early), chunks - 1)
+        first = per_step * (c - early)
+        each(per_step, lambda i: pl.when(first + i < c)(lambda: finish(first + i)))
+
+    each(late_steps, late)
+    done = min(per_step * late_steps, chunks - 1)
     each(chunks - done, lambda i: finish(done + i))
 
     for off in range(1, tensor):
@@ -317,6 +321,36 @@
             send_term(c, (col + off) % tensor).wait_send()
 
     each(chunks, settle_chunk)
+
+
+def write_kernel(blended, activated, blended_out, activated_out, sems):
+    count = sems.shape[0] - 1
+    span = blended.shape[0] // count
+    copies = [
+        pltpu.make_async_copy(
+            blended.at[pl.ds(i * span, span)], blended_out.at[pl.ds(i * span, span)], sems.at[i]
+        )
+        for i in range(count)
+    ]
+    copies.append(pltpu.make_async_copy(activated, activated_out, sems.at[count]))
+    for copy in copies:
+        copy.start()
+    for copy in copies:
+        copy.wait()
+
+
+def write(blended, activated):
+    return pl.pallas_call(
+        write_kernel,
+        out_shape=[
+            jax.ShapeDtypeStruct(blended.shape, blended.dtype),
+            jax.ShapeDtypeStruct(activated.shape, activated.dtype),
+        ],
+        in_specs=[pl.BlockSpec(memory_space=pltpu.VMEM)] * 2,
+        out_specs=[pl.BlockSpec(memory_space=pltpu.HBM)] * 2,
+        scratch_shapes=[pltpu.SemaphoreType.DMA((blended.shape[0] // 2 + 1,))],
+        compiler_params=pltpu.CompilerParams(vmem_limit_bytes=16 * 1024 * 1024),
+    )(blended, activated)
 
 
 def fused(policy, ref_weight, tokens, gain, dp, tensor, chunks, model):
@@ -382,6 +416,7 @@
         tokens,
         gain.reshape(1, features),
     )
+    blended, activated = write(blended, activated)
     return blended.reshape(local, columns), activated
 
 
@@ -415,8 +450,7 @@
             and policy.shape[1] % 16 == 0
             and tokens.shape[1] % 16 == 0
             and columns % 256 == 0
-            and chunks > dp // 2
-            and dp // 2 >= AHEAD
+            and HOP_STEPS * (dp // 2 - 1) in range(AHEAD, chunks)
         )
         if fits:
             return fused(policy, ref_weight, tokens, gain, dp, tensor, chunks, model)

time: 225 us -> 224 us (level)
  local copies, waits for them, and re-layouts: 14.2 us -> 1.69 us
  Pallas kernels: 210 us -> 221 us
    unnamed x8 -> x4, local copies, waits for them, and re-layouts: 14.2 us -> 1.69 us
    pallas_call x1, Pallas kernels: 210 us -> 217 us  [fused(): pl.pallas_call(functools.partial(fused_kernel, plan), out_shape=[jax.Shap...]
    pallas_call x0 -> x1, Pallas kernels: none -> 3.57 us  [write(): pl.pallas_call(write_kernel, out_shape=[jax.ShapeDtypeStruct(blended.shap...]
where the time goes in v3:
time: 224 us; the launch traced here: 223 us
  Pallas kernels  221 us (99%)
    pallas_call x1, Pallas kernels, fused(): pl.pallas_call(functools.partial(fused_kernel, plan), out_shape=[jax.Shap...  217 us

profile of v3, /device:TPU:13, one launch (start us, length us, event | category | flops | bytes accessed | tf_op | source)
XLA Modules:
  0.0 223.0 jit_solution(3058301525278518034)
XLA Ops:
  0.6 0.0 copy-start
  0.6 1.0 copy-done
  1.6 0.0 copy-start.1
  1.6 0.7 copy-done.1
  2.3 217.1 %shard_map.59 = (bf16[8,256,2048]{2,1,0:T(8,128)(2,1)S(1)}, bf16[2,96,2048]{2,1,0:T(8,128)(2,1)S(1)}) custom-call(bf16[256,16384]{1,0:T(8,128)(2,1)} %bitcast.5, bf16[8,256,2048]{2,1,0:T(8,128)(2,1)} %bitcast.6, bf16[2,48,2048]{2,1,0:T(8,128)(2,1)S(1)} %copy-done, f32[1,2048]{1,0:T(1,128)S(1)} %bitcast.4), custom_call_target="tpu_custom_call" | custom-call | flops 6442450944 | bytes 41943040 | tf_op jit(solution)/shard_map/pallas_call | solution.py:366
  219.4 3.6 %shard_map.60 = (bf16[8,256,2048]{2,1,0:T(8,128)(2,1)}, bf16[2,96,2048]{2,1,0:T(8,128)(2,1)}) custom-call(bf16[8,256,2048]{2,1,0:T(8,128)(2,1)S(1)} %get-tuple-element.6.blended, bf16[2,96,2048]{2,1,0:T(8,128)(2,1)S(1)} %get-tuple-element.7.activated), custom_call_target="tpu_custom_call" | custom-call | tf_op jit(solution)/shard_map/pallas_call | solution.py:343
Async XLA Ops:
  0.6 1.0 copy-start
  1.6 0.7 copy-start.1

commit v4 on v3

--- a/solution.py
+++ b/solution.py
@@ -11,7 +11,7 @@
 MESH = pl.DeviceIdType.MESH
 LANES = 128
 AHEAD = 2
-HOP_STEPS = 2
+HOP_STEPS = 1
 
 ema_rate = 0.5
 norm_eps = 1e-06
@@ -179,11 +179,14 @@
     for off in range(1, tensor):
         send_squares((col + off) % tensor).start()
 
-    order = sorted(range(1, dp), key=lambda off: abs(off - dp // 2))
+    half = dp // 2
+    side = me // half
 
     def send_chunk(c):
-        for off in order:
-            send_piece(c, (me + off) % dp).start()
+        for i in range(half):
+            send_piece(c, (1 - side) * half + (me + i) % half).start()
+        for i in range(1, half):
+            send_piece(c, side * half + (me + i) % half).start()
 
     send_chunk(0)
 
@@ -281,14 +284,14 @@
                     part_of(c),
                 ] = result[m * per_micro : (m + 1) * per_micro]
 
-    early = HOP_STEPS * (levels - 1)
+    early = HOP_STEPS * (levels - 1) + 1
     late_steps = chunks - early
     per_step = -(-early // late_steps)
     for c in range(early):
         if c + AHEAD < chunks:
             send_chunk(c + AHEAD)
         take_chunk(c)
-        if c % HOP_STEPS == 0:
+        if c % HOP_STEPS == 0 and c < early - 1:
             relay(c // HOP_STEPS + 1, forward)
     each(levels, lambda z: block_copy(2 * z + 1 - core, pair_send.at[z], pair).wait_recv())
     each(early, multiply)
@@ -450,7 +453,7 @@
             and policy.shape[1] % 16 == 0
             and tokens.shape[1] % 16 == 0
             and columns % 256 == 0
-            and HOP_STEPS * (dp // 2 - 1) in range(AHEAD, chunks)
+            and HOP_STEPS * (dp // 2 - 1) + 1 in range(AHEAD, chunks)
         )
         if fits:
             return fused(policy, ref_weight, tokens, gain, dp, tensor, chunks, model)

time: 224 us -> 218 us (0.973)
  Pallas kernels: 221 us -> 214 us
    pallas_call x1, Pallas kernels: 217 us -> 210 us  [fused(): pl.pallas_call(functools.partial(fused_kernel, plan), out_shape=[jax.Shap...]
where the time goes in v4:
time: 218 us; the launch traced here: 216 us
  Pallas kernels  214 us (98%)
    pallas_call x1, Pallas kernels, fused(): pl.pallas_call(functools.partial(fused_kernel, plan), out_shape=[jax.Shap...  210 us

profile of v4, /device:TPU:13, one launch (start us, length us, event | category | flops | bytes accessed | tf_op | source)
XLA Modules:
  0.0 216.0 jit_solution(3621367376246458604)
XLA Ops:
  0.6 0.0 copy-start
  0.6 1.0 copy-done
  1.6 0.0 copy-start.1
  1.6 0.7 copy-done.1
  2.3 210.1 %shard_map.59 = (bf16[8,256,2048]{2,1,0:T(8,128)(2,1)S(1)}, bf16[2,96,2048]{2,1,0:T(8,128)(2,1)S(1)}) custom-call(bf16[256,16384]{1,0:T(8,128)(2,1)} %bitcast.5, bf16[8,256,2048]{2,1,0:T(8,128)(2,1)} %bitcast.6, bf16[2,48,2048]{2,1,0:T(8,128)(2,1)S(1)} %copy-done, f32[1,2048]{1,0:T(1,128)S(1)} %bitcast.4), custom_call_target="tpu_custom_call" | custom-call | flops 6442450944 | bytes 41943040 | tf_op jit(solution)/shard_map/pallas_call | solution.py:369
  212.4 3.6 %shard_map.60 = (bf16[8,256,2048]{2,1,0:T(8,128)(2,1)}, bf16[2,96,2048]{2,1,0:T(8,128)(2,1)}) custom-call(bf16[8,256,2048]{2,1,0:T(8,128)(2,1)S(1)} %get-tuple-element.6.blended, bf16[2,96,2048]{2,1,0:T(8,128)(2,1)S(1)} %get-tuple-element.7.activated), custom_call_target="tpu_custom_call" | custom-call | tf_op jit(solution)/shard_map/pallas_call | solution.py:346
Async XLA Ops:
  0.6 1.0 copy-start
  1.6 0.7 copy-start.1

commit v5 on v4

--- a/solution.py
+++ b/solution.py
@@ -10,7 +10,7 @@
 
 MESH = pl.DeviceIdType.MESH
 LANES = 128
-AHEAD = 2
+AHEAD = 3
 HOP_STEPS = 1
 
 ema_rate = 0.5
@@ -351,7 +351,7 @@
         ],
         in_specs=[pl.BlockSpec(memory_space=pltpu.VMEM)] * 2,
         out_specs=[pl.BlockSpec(memory_space=pltpu.HBM)] * 2,
-        scratch_shapes=[pltpu.SemaphoreType.DMA((blended.shape[0] // 2 + 1,))],
+        scratch_shapes=[pltpu.SemaphoreType.DMA((blended.shape[0] + 1,))],
         compiler_params=pltpu.CompilerParams(vmem_limit_bytes=16 * 1024 * 1024),
     )(blended, activated)
 

time: 218 us -> 219 us (level)
  no operation moved by 1% of the time
where the time goes in v5:
time: 219 us; the launch traced here: 216 us
  Pallas kernels  214 us (98%)
    pallas_call x1, Pallas kernels, fused(): pl.pallas_call(functools.partial(fused_kernel, plan), out_shape=[jax.Shap...  210 us

profile of v5, /device:TPU:13, one launch (start us, length us, event | category | flops | bytes accessed | tf_op | source)
XLA Modules:
  0.0 216.0 jit_solution(9123146843894143562)
XLA Ops:
  0.6 0.0 copy-start
  0.6 1.0 copy-done
  1.6 0.0 copy-start.1
  1.6 0.7 copy-done.1
  2.3 210.1 %shard_map.59 = (bf16[8,256,2048]{2,1,0:T(8,128)(2,1)S(1)}, bf16[2,96,2048]{2,1,0:T(8,128)(2,1)S(1)}) custom-call(bf16[256,16384]{1,0:T(8,128)(2,1)} %bitcast.5, bf16[8,256,2048]{2,1,0:T(8,128)(2,1)} %bitcast.6, bf16[2,48,2048]{2,1,0:T(8,128)(2,1)S(1)} %copy-done, f32[1,2048]{1,0:T(1,128)S(1)} %bitcast.4), custom_call_target="tpu_custom_call" | custom-call | flops 6442450944 | bytes 41943040 | tf_op jit(solution)/shard_map/pallas_call | solution.py:369
  212.4 3.6 %shard_map.60 = (bf16[8,256,2048]{2,1,0:T(8,128)(2,1)}, bf16[2,96,2048]{2,1,0:T(8,128)(2,1)}) custom-call(bf16[8,256,2048]{2,1,0:T(8,128)(2,1)S(1)} %get-tuple-element.6.blended, bf16[2,96,2048]{2,1,0:T(8,128)(2,1)S(1)} %get-tuple-element.7.activated), custom_call_target="tpu_custom_call" | custom-call | tf_op jit(solution)/shard_map/pallas_call | solution.py:346
Async XLA Ops:
  0.6 1.0 copy-start
  1.6 0.7 copy-start.1

commit v6 on v5

--- a/solution.py
+++ b/solution.py
@@ -73,6 +73,21 @@
             barrier, inc=1, device_id={"tensor": (col + off) % tensor}, device_id_type=MESH
         )
 
+    parts = chunks + 1
+
+    def lanes_of(c):
+        if isinstance(c, int) and c >= chunks - 1:
+            return chunks - 1, (c - chunks + 1) * (width // 2), width // 2
+        return c, 0, width
+
+    def columns_of(c):
+        chunk, first, size = lanes_of(c)
+        return pl.ds(pl.multiple_of(chunk * width + first, 128), size)
+
+    def buffer_lanes(c):
+        chunk, first, size = lanes_of(c)
+        return chunk, pl.ds(first, size)
+
     def own_piece(c):
         return pltpu.make_async_copy(
             policy.at[:, pl.ds(pl.multiple_of(me * columns + c * width, width), width)],
@@ -89,11 +104,12 @@
         )
 
     def send_piece(c, other):
-        return pltpu.make_async_remote_copy(
-            src_ref=policy.at[
-                :, pl.ds(pl.multiple_of(other * columns + c * width, width), width)
-            ],
-            dst_ref=arrived.at[c, me],
+        chunk, lanes = buffer_lanes(c)
+        _, first, size = lanes_of(c)
+        start = pl.multiple_of(other * columns + chunk * width + first, 128)
+        return pltpu.make_async_remote_copy(
+            src_ref=policy.at[:, pl.ds(start, size)],
+            dst_ref=arrived.at[chunk, me, :, lanes],
             send_sem=piece_send.at[c, other],
             recv_sem=piece_recv.at[c, me],
             device_id={"dp": other},
@@ -101,9 +117,10 @@
         )
 
     def take_piece(c, other):
-        return pltpu.make_async_remote_copy(
-            src_ref=policy.at[:, pl.ds(0, width)],
-            dst_ref=arrived.at[c, other],
+        chunk, lanes = buffer_lanes(c)
+        return pltpu.make_async_remote_copy(
+            src_ref=policy.at[:, pl.ds(0, lanes_of(c)[2])],
+            dst_ref=arrived.at[chunk, other, :, lanes],
             send_sem=piece_send.at[c, other],
             recv_sem=piece_recv.at[c, other],
             device_id={"dp": other},
@@ -141,9 +158,10 @@
         )
 
     def send_term(c, other):
-        return pltpu.make_async_remote_copy(
-            src_ref=partial.at[c, pl.ds(other * per_owner, per_owner)],
-            dst_ref=terms.at[c, col],
+        chunk, lanes = buffer_lanes(c)
+        return pltpu.make_async_remote_copy(
+            src_ref=partial.at[chunk, pl.ds(other * per_owner, per_owner), :, lanes],
+            dst_ref=terms.at[chunk, col, :, :, lanes],
             send_sem=term_send.at[c, other],
             recv_sem=term_recv.at[c, col],
             device_id={"tensor": other},
@@ -151,9 +169,10 @@
         )
 
     def take_term(c, other):
-        return pltpu.make_async_remote_copy(
-            src_ref=partial.at[c, pl.ds(other * per_owner, per_owner)],
-            dst_ref=terms.at[c, other],
+        chunk, lanes = buffer_lanes(c)
+        return pltpu.make_async_remote_copy(
+            src_ref=partial.at[chunk, pl.ds(other * per_owner, per_owner), :, lanes],
+            dst_ref=terms.at[chunk, other, :, :, lanes],
             send_sem=term_send.at[c, other],
             recv_sem=term_recv.at[c, other],
             device_id={"tensor": other},
@@ -242,13 +261,15 @@
         send_chunk(c)
 
     def take_chunk(c):
-        ref_piece(c).wait()
-        own_piece(c).wait()
+        chunk, lanes = buffer_lanes(c)
+        if c < chunks:
+            ref_piece(chunk).wait()
+            own_piece(chunk).wait()
 
         def blend(d):
-            old = blended[d, :, part_of(c)].astype(jnp.float32)
-            new = arrived[c, d].astype(jnp.float32)
-            blended[d, :, part_of(c)] = (old + ema_rate * (new - old)).astype(jnp.bfloat16)
+            old = blended[d, :, columns_of(c)].astype(jnp.float32)
+            new = arrived[chunk, d, :, lanes].astype(jnp.float32)
+            blended[d, :, columns_of(c)] = (old + ema_rate * (new - old)).astype(jnp.bfloat16)
 
         blend(me)
 
@@ -263,32 +284,33 @@
 
     def multiply(c):
         left = gathered[...].reshape(dp * rows, features)
-        right = blended[:, :, part_of(c)].reshape(features, width)
+        chunk, lanes = buffer_lanes(c)
+        size = lanes_of(c)[2]
+        right = blended[:, :, columns_of(c)].reshape(features, size)
         product = jnp.dot(left, right, preferred_element_type=jnp.float32) * out_scale
-        partial[c] = product.astype(jnp.bfloat16).reshape(dp, rows, width)
+        partial[chunk, :, :, lanes] = product.astype(jnp.bfloat16).reshape(dp, rows, size)
         for off in range(1, tensor):
             send_term(c, (col + off) % tensor).start()
 
     def finish(c):
+        chunk, lanes = buffer_lanes(c)
         for off in range(1, tensor):
             take_term(c, (col + off) % tensor).wait_recv()
         for b in range(per_owner):
-            gate = partial[c, col * per_owner + b].astype(jnp.float32)
+            gate = partial[chunk, col * per_owner + b, :, lanes].astype(jnp.float32)
             for off in range(1, tensor):
-                gate = gate + terms[c, (col + off) % tensor, b].astype(jnp.float32)
+                gate = gate + terms[chunk, (col + off) % tensor, b, :, lanes].astype(jnp.float32)
             result = (gate / (1.0 + jnp.exp(-gate))).astype(jnp.bfloat16)
             for m in range(micros):
                 activated[
                     m,
                     pl.ds(b * per_micro, per_micro),
-                    part_of(c),
+                    columns_of(c),
                 ] = result[m * per_micro : (m + 1) * per_micro]
 
     early = HOP_STEPS * (levels - 1) + 1
-    late_steps = chunks - early
-    per_step = -(-early // late_steps)
     for c in range(early):
-        if c + AHEAD < chunks:
+        if c + AHEAD < parts:
             send_chunk(c + AHEAD)
         take_chunk(c)
         if c % HOP_STEPS == 0 and c < early - 1:
@@ -296,21 +318,14 @@
     each(levels, lambda z: block_copy(2 * z + 1 - core, pair_send.at[z], pair).wait_recv())
     each(early, multiply)
 
-    def late(c):
-        c = c + early
-
-        @pl.when(c + AHEAD < chunks)
-        def _():
+    for c in range(early, parts):
+        if c + AHEAD < parts:
             send_chunk(c + AHEAD)
-
         take_chunk(c)
         multiply(c)
-        first = per_step * (c - early)
-        each(per_step, lambda i: pl.when(first + i < c)(lambda: finish(first + i)))
-
-    each(late_steps, late)
-    done = min(per_step * late_steps, chunks - 1)
-    each(chunks - done, lambda i: finish(done + i))
+        finish(c - early)
+    for c in range(parts - early, parts):
+        finish(c)
 
     for off in range(1, tensor):
         send_squares((col + off) % tensor).wait_send()
@@ -323,7 +338,9 @@
         for off in range(1, tensor):
             send_term(c, (col + off) % tensor).wait_send()
 
-    each(chunks, settle_chunk)
+    each(chunks - 1, settle_chunk)
+    for c in range(chunks - 1, parts):
+        settle_chunk(c)
 
 
 def write_kernel(blended, activated, blended_out, activated_out, sems):
@@ -390,8 +407,8 @@
             pltpu.VMEM((dp, rows, features), bf16),
             pltpu.VMEM((chunks, dp, rows, width), bf16),
             pltpu.VMEM((chunks, tensor, per_owner, rows, width), bf16),
-            dma((chunks, dp)),
-            dma((chunks, dp)),
+            dma((chunks + 1, dp)),
+            dma((chunks + 1, dp)),
             dma((chunks,)),
             dma((chunks,)),
             dma,
@@ -402,8 +419,8 @@
             dma((dp // 2,)),
             dma((dp // 2,)),
             dma((dp,)),
-            dma((chunks, tensor)),
-            dma((chunks, tensor)),
+            dma((chunks + 1, tensor)),
+            dma((chunks + 1, tensor)),
         ],
         compiler_params=pltpu.CompilerParams(
             collective_id=0, has_side_effects=True, vmem_limit_bytes=40 * 1024 * 1024

time: 219 us -> 219 us (level)
  no operation moved by 1% of the time
where the time goes in v6:
time: 219 us; the launch traced here: 216 us
  Pallas kernels  213 us (97%)
    pallas_call x1, Pallas kernels, fused(): pl.pallas_call(functools.partial(fused_kernel, plan), out_shape=[jax.Shap...  210 us

profile of v6, /device:TPU:13, one launch (start us, length us, event | category | flops | bytes accessed | tf_op | source)
XLA Modules:
  0.0 215.8 jit_solution(1274152644777757642)
XLA Ops:
  0.6 0.0 copy-start
  0.6 1.0 copy-done
  1.6 0.0 copy-start.1
  1.6 0.7 copy-done.1
  2.3 209.8 %shard_map.59 = (bf16[8,256,2048]{2,1,0:T(8,128)(2,1)S(1)}, bf16[2,96,2048]{2,1,0:T(8,128)(2,1)S(1)}) custom-call(bf16[256,16384]{1,0:T(8,128)(2,1)} %bitcast.5, bf16[8,256,2048]{2,1,0:T(8,128)(2,1)} %bitcast.6, bf16[2,48,2048]{2,1,0:T(8,128)(2,1)S(1)} %copy-done, f32[1,2048]{1,0:T(1,128)S(1)} %bitcast.4), custom_call_target="tpu_custom_call" | custom-call | flops 6442450944 | bytes 41943040 | tf_op jit(solution)/shard_map/pallas_call | solution.py:386
  212.2 3.6 %shard_map.60 = (bf16[8,256,2048]{2,1,0:T(8,128)(2,1)}, bf16[2,96,2048]{2,1,0:T(8,128)(2,1)}) custom-call(bf16[8,256,2048]{2,1,0:T(8,128)(2,1)S(1)} %get-tuple-element.6.blended, bf16[2,96,2048]{2,1,0:T(8,128)(2,1)S(1)} %get-tuple-element.7.activated), custom_call_target="tpu_custom_call" | custom-call | tf_op jit(solution)/shard_map/pallas_call | solution.py:363
Async XLA Ops:
  0.6 1.0 copy-start
  1.6 0.7 copy-start.1

commit v7 on v5

--- a/solution.py
+++ b/solution.py
@@ -184,7 +184,7 @@
 
     def send_chunk(c):
         for i in range(half):
-            send_piece(c, (1 - side) * half + (me + i) % half).start()
+            send_piece(c, (1 - side) * half + (me + i + c) % half).start()
         for i in range(1, half):
             send_piece(c, side * half + (me + i) % half).start()
 

time: 219 us -> 218 us (level); the launches traced: 216 us -> 217 us
  no operation moved by 1% of the time
where the time goes in v7:
time: 218 us; the launch traced here: 217 us
  Pallas kernels  215 us (99%)
    pallas_call x1, Pallas kernels, fused(): pl.pallas_call(functools.partial(fused_kernel, plan), out_shape=[jax.Shap...  211 us

profile of v7, /device:TPU:13, one launch (start us, length us, event | category | flops | bytes accessed | tf_op | source)
XLA Modules:
  0.0 217.3 jit_solution(4955463897981764981)
XLA Ops:
  0.6 0.0 copy-start
  0.6 1.0 copy-done
  1.6 0.0 copy-start.1
  1.6 0.7 copy-done.1
  2.3 211.4 %shard_map.59 = (bf16[8,256,2048]{2,1,0:T(8,128)(2,1)S(1)}, bf16[2,96,2048]{2,1,0:T(8,128)(2,1)S(1)}) custom-call(bf16[256,16384]{1,0:T(8,128)(2,1)} %bitcast.5, bf16[8,256,2048]{2,1,0:T(8,128)(2,1)} %bitcast.6, bf16[2,48,2048]{2,1,0:T(8,128)(2,1)S(1)} %copy-done, f32[1,2048]{1,0:T(1,128)S(1)} %bitcast.4), custom_call_target="tpu_custom_call" | custom-call | flops 6442450944 | bytes 41943040 | tf_op jit(solution)/shard_map/pallas_call | solution.py:369
  213.7 3.6 %shard_map.60 = (bf16[8,256,2048]{2,1,0:T(8,128)(2,1)}, bf16[2,96,2048]{2,1,0:T(8,128)(2,1)}) custom-call(bf16[8,256,2048]{2,1,0:T(8,128)(2,1)S(1)} %get-tuple-element.6.blended, bf16[2,96,2048]{2,1,0:T(8,128)(2,1)S(1)} %get-tuple-element.7.activated), custom_call_target="tpu_custom_call" | custom-call | tf_op jit(solution)/shard_map/pallas_call | solution.py:346
Async XLA Ops:
  0.6 1.0 copy-start
  1.6 0.7 copy-start.1
